TPU v7x, 128 devices: a whole 4x4x4 slice. The times are simulated.
128 devices in a mesh: freq: 8 (over x, y_lo), mat: 16 (over z, y_hi, core).
Axes of the slice: x: 4, y: 4 (y_hi: 2, y_lo: 2; y = y_hi * 2 + y_lo), z: 4, core: 2. Of those that a mesh axis runs over, the one named last changes fastest.
Arguments:
- traces: bfloat16 [2048, 64, 4096], P('freq', None, 'mat'), may hold values from -6 to 6
- reflection: bfloat16 [16, 2, 4096, 4096], P('freq', None, 'mat'), may hold values from -0.0625 to 0.0625
- onset: int32 [64, 4096], P(None, 'mat'), may hold values from 512 to 2047
Outputs:
- windowed: bfloat16 [2048, 64, 4096], P('freq', None, 'mat')
Inputs may be any that keep to these rules, and one draw needn't show every extreme that they name: onset sample of the direct arrival for each focal point and receiver.
All inputs are finite; a program needn't handle non-finite values.
Results may differ from a plain program's by a relative error of at most 0.0069.
Values may be sent and summed in bfloat16 or wider, within the bound.
A program may use at most 128 MiB of HBM per device.

v0:
```python
import math

import jax
import jax.numpy as jnp
from jax import lax
from jax.sharding import PartitionSpec as P


def forward_table(base_band, first_band, band_count, sample_time_count, sampling_interval):
    angular_freq_list = base_band + first_band + jnp.arange(band_count, dtype=jnp.int32)
    sample_moments = jnp.arange(sample_time_count, dtype=jnp.int32)
    phase_angles = (
        angular_freq_list[:, None] * sample_moments[None, :] % sampling_interval
    ).astype(jnp.float32) * (2.0 * math.pi / sampling_interval)
    factor = 1.0 / math.sqrt(sampling_interval)
    table = jnp.stack([jnp.cos(phase_angles) * factor, -jnp.sin(phase_angles) * factor], axis=1)
    return table.reshape(2 * band_count, sample_time_count).astype(jnp.bfloat16)


def inverse_table(
    base_band,
    first_band,
    band_count,
    earliest_sample_time,
    sample_time_count,
    sampling_interval,
    bands_total,
):
    angular_freq_list = base_band + first_band + jnp.arange(band_count, dtype=jnp.int32)
    sample_moments = earliest_sample_time + jnp.arange(sample_time_count, dtype=jnp.int32)
    phase_angles = (
        sample_moments[:, None] * angular_freq_list[None, :] % sampling_interval
    ).astype(jnp.float32) * (2.0 * math.pi / sampling_interval)
    factor = 1.0 / math.sqrt(bands_total)
    table = jnp.stack([jnp.cos(phase_angles) * factor, -jnp.sin(phase_angles) * factor], axis=2)
    return table.reshape(sample_time_count, 2 * band_count).astype(jnp.bfloat16)


def accumulate(reflection, panels):
    return jnp.einsum("kcpw,kdrw->kcpdr", panels, reflection, preferred_element_type=jnp.float32)


def on_device(traces, reflection, onset):
    temporal_rows, focal_count, recv_rows = traces.shape
    freq_devices = lax.axis_size("freq")
    sampling_interval = temporal_rows * freq_devices
    per_device = reflection.shape[0]
    bands_total = per_device * freq_devices
    base_band = sampling_interval // 16
    earliest_sample_time = lax.axis_index("freq") * temporal_rows
    gathered = lax.all_to_all(traces, "freq", split_axis=1, concat_axis=0, tiled=True)
    forward = forward_table(base_band, 0, bands_total, sampling_interval, sampling_interval)
    local_spectra = jnp.dot(
        forward, gathered.reshape(sampling_interval, -1), preferred_element_type=jnp.float32
    )
    local_spectra = local_spectra.astype(jnp.bfloat16).reshape(
        bands_total, 2, focal_count // freq_devices, recv_rows
    )
    spectra = lax.all_to_all(local_spectra, "freq", split_axis=0, concat_axis=2, tiled=True)
    products = accumulate(reflection, lax.all_gather(spectra, "mat", axis=3, tiled=True))
    real_part = products[:, 0, :, 0] - products[:, 1, :, 1]
    imag_part = products[:, 1, :, 0] + products[:, 0, :, 1]
    response = jnp.stack([real_part, imag_part], axis=1).astype(jnp.bfloat16)
    pieces = lax.all_gather(response, "freq", axis=0, tiled=True)
    piece_bands = pieces.shape[0]
    table = inverse_table(
        base_band,
        jnp.int32(0),
        piece_bands,
        earliest_sample_time,
        temporal_rows,
        sampling_interval,
        bands_total,
    )
    wavelet_trace = jnp.dot(
        table, pieces.reshape(2 * piece_bands, -1), preferred_element_type=jnp.float32
    )
    wavelet_trace = wavelet_trace.reshape(temporal_rows, focal_count, recv_rows)
    sample_moments = earliest_sample_time + jnp.arange(temporal_rows, dtype=jnp.int32)
    return jnp.where(sample_moments[:, None, None] < onset[None], wavelet_trace, 0.0).astype(
        jnp.bfloat16
    )


def solution(mesh):
    placed = (P("freq", None, "mat"), P("freq", None, "mat", None), P(None, "mat"))
    return jax.shard_map(
        on_device, mesh=mesh, in_specs=placed, out_specs=P("freq", None, "mat"), check_vma=False
    )
```

profile of v0, /device:TPU:1, one launch (start us, length us, event | category | flops | bytes accessed | tf_op | source)
XLA Modules:
  0.0 290.4 jit_solution(8987665596310700736)
XLA Ops:
  6.5 11.5 %copy.33 = bf16[256,64,256]{2,0,1:T(8,128)(2,1)} copy(bf16[256,64,256]{2,1,0:T(8,128)(2,1)} %param.3) | data formatting | bytes 16777216 | tf_op args[0]
  18.1 5.9 %all-to-all-start = ((bf16[256,64,256]{2,0,1:T(8,128)(2,1)}), bf16[256,64,256]{2,0,1:T(8,128)(2,1)}, u32[]{:S(2)}, u32[]{:S(2)}) async-start(bf16[256,64,256]{2,0,1:T(8,128)(2,1)} %copy.33), calls=%async_computation | async-start | bytes 16777216 | tf_op jit(solution)/shard_map/all_to_all | solution.py:51
  23.9 0.2 all-gather.3.cloned.1.call-start
  24.2 0.6 multiply_convert_fusion.1
  24.8 0.1 copy.32
  25.0 0.1 convert_element_type.60
  25.0 114.0 %all-to-all-done = bf16[256,64,256]{2,0,1:T(8,128)(2,1)} async-done(((bf16[256,64,256]{2,0,1:T(8,128)(2,1)}), bf16[256,64,256]{2,0,1:T(8,128)(2,1)}, u32[]{:S(2)}, u32[]{:S(2)}) %all-to-all-start) | async-done | bytes 8388640 | tf_op jit(solution)/shard_map/all_to_all | solution.py:51
  139.1 11.9 %copy.34 = bf16[256,8,8,256]{3,2,0,1:T(8,128)(2,1)} copy(bf16[256,8,8,256]{3,0,2,1:T(8,128)(2,1)} %bitcast) | data formatting | bytes 16777216 | tf_op jit(solution)/shard_map/all_to_all | solution.py:51
  151.0 10.3 %copy.46 = bf16[256,8,8,256]{3,1,2,0:T(8,128)(2,1)} copy(bf16[256,8,8,256]{3,2,1,0:T(8,128)(2,1)} %bitcast.60) | data formatting | bytes 16777216
  161.3 4.9 %convolution_convert_fusion = bf16[32,2048]{1,0:T(8,128)(2,1)S(1)} fusion(bf16[32,2048]{1,0:T(8,128)(2,1)S(1)} %convert_element_type.60, bf16[2048,2048]{1,0:T(8,128)(2,1)} %bitcast.59), kind=kOutput, calls=%fused_computation.3 | convolution fusion | flops 268500992 | bytes 8650752 | tf_op jit(solution)/shard_map/dot_general | solution.py:53
  166.2 0.0 copy-start
  166.3 8.1 %all_to_all.33 = bf16[16,2,8,256]{3,2,1,0:T(8,128)(2,1)S(1)} all-to-all(bf16[16,2,8,256]{3,2,1,0:T(8,128)(2,1)S(1)} %bitcast.64), channel_id=1, replica_groups=mesh['freq'=8,'mat'=16] {'freq'}, dimensions={0} | all-to-all | bytes 262144 | tf_op jit(solution)/shard_map/all_to_all | solution.py:59
  174.3 0.7 copy.57
  175.0 0.0 all-gather.3.cloned.1.call-update
  175.0 0.3 all-gather.5.cloned.1.call-start
  175.3 50.8 %all-gather.3.cloned.1.call-done = bf16[2,2,64,4096]{3,2,1,0:T(8,128)(2,1)} async-done(((bf16[2,2,64,256]{3,2,1,0:T(8,128)(2,1)}), bf16[2,2,64,4096]{3,2,1,0:T(8,128)(2,1)}) %all-gather.3.cloned.1.call-update) | async-done | bytes 2097168 | tf_op jit(solution)/shard_map/all_gather | solution.py:60
  226.1 6.9 %fusion = f32[2,2,64,2,256]{4,2,3,1,0:T(8,128)S(1)} fusion(bf16[2,2,256,4096]{3,2,1,0:T(8,128)(2,1)} %param.4, bf16[2,2,64,4096]{3,2,1,0:T(8,128)(2,1)} %all-gather.3.cloned.1.call-done), kind=kOutput, calls=%fused_computation.1 | convolution fusion | flops 1073741824 | bytes 11010048 | tf_op jit(solution)/shard_map/kcpw,kdrw->kcpdr/dot_general | solution.py:40
  233.1 0.7 pad_maximum_fusion.1
  233.8 0.0 all-gather.5.cloned.1.call-update
  233.8 0.2 multiply_convert_fusion.3
  234.0 32.1 %all-gather.5.cloned.1.call-done = bf16[16,2,64,256]{3,2,0,1:T(8,128)(2,1)} async-done(((bf16[2,2,64,256]{3,2,0,1:T(8,128)(2,1)}), bf16[16,2,64,256]{3,2,0,1:T(8,128)(2,1)}) %all-gather.5.cloned.1.call-update) | async-done | bytes 1048592 | tf_op jit(solution)/shard_map/all_gather | solution.py:64
  266.1 1.3 copy.38
  267.3 0.0 copy-done
  267.4 4.7 %select_convert_fusion = bf16[256,64,256]{2,0,1:T(8,128)(2,1)} fusion(bf16[256,32,1]{0,1,2:T(8,128)(2,1)S(1)} %reshape.327, s32[64,256]{1,0:T(8,128)S(1)} %copy-done, s32[256]{0:T(256)S(1)} %iota_add_fusion, bf16[4,8,64,256]{3,2,1,0:T(8,128)(2,1)S(1)} %bitcast.61), kind=kOutput, calls=%fused_computation | convolution fusion | flops 281018368 | bytes 9520128 | tf_op jit(solution)/shard_map/dot_general | solution.py:75
  272.0 11.5 %copy.40 = bf16[256,64,256]{2,1,0:T(8,128)(2,1)} copy(bf16[256,64,256]{2,0,1:T(8,128)(2,1)} %select_convert_fusion) | data formatting | bytes 16777216 | tf_op jit(solution)/shard_map/convert_element_type | solution.py:80
  (9 shorter events, 0.1 us)
Async XLA Ops:
  18.1 121.0 %all-to-all-start = ((bf16[256,64,256]{2,0,1:T(8,128)(2,1)}), bf16[256,64,256]{2,0,1:T(8,128)(2,1)}, u32[]{:S(2)}, u32[]{:S(2)}) async-start(bf16[256,64,256]{2,0,1:T(8,128)(2,1)} %copy.33), calls=%async_computation | async-start | bytes 16777216 | tf_op jit(solution)/shard_map/all_to_all | solution.py:51
  23.9 202.1 %all-gather.3.cloned.1.call-start = ((), (), s32[]{:S(2)}) async-start(), calls=%async_computation.2 | async-start | bytes 2228224 | tf_op jit(solution)/shard_map/all_gather | solution.py:60
  166.2 101.1 %copy-start = (s32[64,256]{1,0:T(8,128)S(1)}, s32[64,256]{1,0:T(8,128)}, u32[]{:S(2)}) copy-start(s32[64,256]{1,0:T(8,128)} %param.5) | copy-start | bytes 196612
  175.0 91.0 %all-gather.5.cloned.1.call-start = ((), (), s32[]{:S(2)}) async-start(), calls=%async_computation.3 | async-start | bytes 1179648 | tf_op jit(solution)/shard_map/all_gather | solution.py:64
Sparse Core Ops, SparseCore 0:
  175.2 50.8 all-gather.2
  233.9 32.1 all-gather.4
where the time goes:
time: 295 us; the launch traced here: 290 us
  waiting for transfers between devices  197 us (67%)
  local copies, waits for them, and re-layouts  47.5 us (16%)
  matrix products  16.5 us (6%)
  between operations  13.5 us (5%)
  blocking collectives  8.09 us (3%)
  starting transfers between devices  6.34 us (2%)
    all_to_all x1, waiting for transfers between devices, on_device(): lax.all_to_all(traces, 'freq', split_axis=1, concat_axis=0, tiled=True)  114 us
    all_gather x1, waiting for transfers between devices, on_device(): lax.all_gather(spectra, 'mat', axis=3, tiled=True)  50.8 us
    all_gather x1, waiting for transfers between devices, on_device(): pieces = lax.all_gather(response, 'freq', axis=0, tiled=True)  32.1 us
    unnamed x5, local copies, waits for them, and re-layouts  21.9 us
    all_to_all x1, local copies, waits for them, and re-layouts, on_device(): lax.all_to_all(traces, 'freq', split_axis=1, concat_axis=0, tiled=True)  11.9 us
    convert_element_type x1, local copies, waits for them, and re-layouts, on_device(): jnp.where(sample_moments[:, None, None] < onset[None], wavelet_trace, 0.0)  11.5 us
    all_to_all x1, blocking collectives, on_device(): lax.all_to_all(local_spectra, 'freq', split_axis=0, concat_axis=2, tiled=...  8.09 us
    dot_general x1, matrix products, accumulate(): jnp.einsum('kcpw,kdrw->kcpdr', panels, reflection, preferred_element_type...  6.94 us
  transfers between devices with their start and end apart: 3, of which 3 were waited for; matrix products, arithmetic and copies ran while one was open for 0% of the time, Pallas kernels for 0%

commit v1 on v0

--- a/solution.py
+++ b/solution.py
@@ -6,9 +6,11 @@
 from jax.sharding import PartitionSpec as P
 
 
-def forward_table(base_band, first_band, band_count, sample_time_count, sampling_interval):
+def forward_table(
+    base_band, first_band, band_count, earliest_sample_time, sample_time_count, sampling_interval
+):
     angular_freq_list = base_band + first_band + jnp.arange(band_count, dtype=jnp.int32)
-    sample_moments = jnp.arange(sample_time_count, dtype=jnp.int32)
+    sample_moments = earliest_sample_time + jnp.arange(sample_time_count, dtype=jnp.int32)
     phase_angles = (
         angular_freq_list[:, None] * sample_moments[None, :] % sampling_interval
     ).astype(jnp.float32) * (2.0 * math.pi / sampling_interval)
@@ -48,15 +50,18 @@
     bands_total = per_device * freq_devices
     base_band = sampling_interval // 16
     earliest_sample_time = lax.axis_index("freq") * temporal_rows
-    gathered = lax.all_to_all(traces, "freq", split_axis=1, concat_axis=0, tiled=True)
-    forward = forward_table(base_band, 0, bands_total, sampling_interval, sampling_interval)
-    local_spectra = jnp.dot(
-        forward, gathered.reshape(sampling_interval, -1), preferred_element_type=jnp.float32
+    earliest = lax.axis_index("freq") * temporal_rows
+    forward = forward_table(
+        base_band, 0, bands_total, earliest, temporal_rows, sampling_interval
     )
-    local_spectra = local_spectra.astype(jnp.bfloat16).reshape(
-        bands_total, 2, focal_count // freq_devices, recv_rows
+    partial = jnp.dot(
+        forward, traces.reshape(temporal_rows, -1), preferred_element_type=jnp.float32
     )
-    spectra = lax.all_to_all(local_spectra, "freq", split_axis=0, concat_axis=2, tiled=True)
+    partial = partial.astype(jnp.bfloat16).reshape(
+        freq_devices, per_device, 2, focal_count, recv_rows
+    )
+    parts = lax.all_to_all(partial, "freq", split_axis=0, concat_axis=0, tiled=True)
+    spectra = jnp.sum(parts.astype(jnp.float32), axis=0).astype(jnp.bfloat16)
     products = accumulate(reflection, lax.all_gather(spectra, "mat", axis=3, tiled=True))
     real_part = products[:, 0, :, 0] - products[:, 1, :, 1]
     imag_part = products[:, 1, :, 0] + products[:, 0, :, 1]

time: 295 us -> 166 us (0.56)
  the two profiles are of different devices: /device:TPU:1 before, /device:TPU:0 now
where the time goes in v1:
time: 166 us
  waiting for transfers between devices  84.8 us (51%)
  local copies, waits for them, and re-layouts  28.6 us (17%)
  blocking collectives  20.7 us (12%)
  matrix products  16.5 us (10%)
  between operations  13.5 us (8%)
  other arithmetic  1.84 us (1%)
    all_gather x1, waiting for transfers between devices, on_device(): lax.all_gather(spectra, 'mat', axis=3, tiled=True)  47.8 us
    all_gather x1, waiting for transfers between devices, on_device(): pieces = lax.all_gather(response, 'freq', axis=0, tiled=True)  37 us
    all_to_all x1, blocking collectives, on_device(): lax.all_to_all(partial, 'freq', split_axis=0, concat_axis=0, tiled=True)  20.7 us
    unnamed x4, local copies, waits for them, and re-layouts  15.7 us
    convert_element_type x1, local copies, waits for them, and re-layouts, on_device(): jnp.where(sample_moments[:, None, None] < onset[None], wavelet_trace, 0.0)  11.5 us
    dot_general x1, matrix products, accumulate(): jnp.einsum('kcpw,kdrw->kcpdr', panels, reflection, preferred_element_type...  6.94 us
    dot_general x1, matrix products, on_device(): jnp.dot(forward, traces.reshape(temporal_rows, -1), preferred_element_typ...  4.92 us
    dot_general x1, matrix products, on_device(): jnp.dot(table, pieces.reshape(2 * piece_bands, -1), preferred_element_typ...  4.66 us
  transfers between devices with their start and end apart: 2, of which 2 were waited for; matrix products, arithmetic and copies ran while one was open for 0% of the time, Pallas kernels for 0%

profile of v1, /device:TPU:0, one launch (start us, length us, event | category | flops | bytes accessed | tf_op | source)
XLA Modules:
  0.0 166.1 jit_solution(9028758283541389684)
XLA Ops:
  6.5 0.0 all-gather.3.cloned.1.call-start
  6.5 0.2 multiply_convert_fusion.1
  6.8 15.4 %copy.29 = bf16[32,8,64,256]{3,1,2,0:T(8,128)(2,1)} copy(bf16[32,8,64,256]{3,2,1,0:T(8,128)(2,1)} %bitcast.51) | data formatting | bytes 16777216
  22.2 4.9 %convolution_convert_fusion = bf16[32,16384]{1,0:T(8,128)(2,1)S(1)} fusion(bf16[32,256]{1,0:T(8,128)(2,1)S(1)} %convert_element_type.60, bf16[256,16384]{1,0:T(8,128)(2,1)} %bitcast.50), kind=kOutput, calls=%fused_computation | convolution fusion | flops 268959744 | bytes 9453568 | tf_op jit(solution)/shard_map/dot_general | solution.py:57
  27.1 0.2 copy.30
  27.3 0.0 copy-start
  27.4 20.7 %all_to_all.5 = bf16[8,2,2,64,256]{4,3,2,1,0:T(8,128)(2,1)S(1)} all-to-all(bf16[8,2,2,64,256]{4,3,2,1,0:T(8,128)(2,1)S(1)} %bitcast.53), channel_id=1, replica_groups=mesh['freq'=8,'mat'=16] {'freq'}, dimensions={0} | all-to-all | bytes 2097152 | tf_op jit(solution)/shard_map/all_to_all | solution.py:63
  48.0 0.8 reduce_sum.12
  48.8 0.0 all-gather.3.cloned.1.call-update
  48.9 0.2 all-gather.5.cloned.1.call-start
  49.1 47.8 %all-gather.3.cloned.1.call-done = bf16[2,2,64,4096]{3,2,1,0:T(8,128)(2,1)} async-done(((bf16[2,2,64,256]{3,2,1,0:T(8,128)(2,1)}), bf16[2,2,64,4096]{3,2,1,0:T(8,128)(2,1)}) %all-gather.3.cloned.1.call-update) | async-done | bytes 2097168 | tf_op jit(solution)/shard_map/all_gather | solution.py:65
  96.9 6.9 %fusion = f32[2,2,64,2,256]{4,2,3,1,0:T(8,128)S(1)} fusion(bf16[2,2,256,4096]{3,2,1,0:T(8,128)(2,1)} %param.4, bf16[2,2,64,4096]{3,2,1,0:T(8,128)(2,1)} %all-gather.3.cloned.1.call-done), kind=kOutput, calls=%fused_computation.2 | convolution fusion | flops 1073741824 | bytes 11010048 | tf_op jit(solution)/shard_map/kcpw,kdrw->kcpdr/dot_general | solution.py:42
  103.9 0.7 pad_maximum_fusion
  104.5 0.0 all-gather.5.cloned.1.call-update
  104.6 0.2 multiply_convert_fusion.3
  104.8 37.0 %all-gather.5.cloned.1.call-done = bf16[16,2,64,256]{3,2,0,1:T(8,128)(2,1)} async-done(((bf16[2,2,64,256]{3,2,0,1:T(8,128)(2,1)}), bf16[16,2,64,256]{3,2,0,1:T(8,128)(2,1)}) %all-gather.5.cloned.1.call-update) | async-done | bytes 1048592 | tf_op jit(solution)/shard_map/all_gather | solution.py:69
  141.8 1.3 copy.21
  143.0 0.0 copy-done
  143.1 4.7 %select_convert_fusion = bf16[256,64,256]{2,0,1:T(8,128)(2,1)} fusion(bf16[256,32,1]{0,1,2:T(8,128)(2,1)S(1)} %reshape.357, s32[64,256]{1,0:T(8,128)S(1)} %copy-done, s32[256]{0:T(256)S(1)} %iota_add_fusion, bf16[4,8,64,256]{3,2,1,0:T(8,128)(2,1)S(1)} %bitcast.54), kind=kOutput, calls=%fused_computation.1 | convolution fusion | flops 281018368 | bytes 9520128 | tf_op jit(solution)/shard_map/dot_general | solution.py:80
  147.7 11.5 %copy.23 = bf16[256,64,256]{2,1,0:T(8,128)(2,1)} copy(bf16[256,64,256]{2,0,1:T(8,128)(2,1)} %select_convert_fusion) | data formatting | bytes 16777216 | tf_op jit(solution)/shard_map/convert_element_type | solution.py:85
  (10 shorter events, 0.1 us)
Async XLA Ops:
  6.5 90.3 %all-gather.3.cloned.1.call-start = ((), (), s32[]{:S(2)}) async-start(), calls=%async_computation.1 | async-start | bytes 2228224 | tf_op jit(solution)/shard_map/all_gather | solution.py:65
  27.3 115.7 %copy-start = (s32[64,256]{1,0:T(8,128)S(1)}, s32[64,256]{1,0:T(8,128)}, u32[]{:S(2)}) copy-start(s32[64,256]{1,0:T(8,128)} %param.5) | copy-start | bytes 196612
  48.9 92.9 %all-gather.5.cloned.1.call-start = ((), (), s32[]{:S(2)}) async-start(), calls=%async_computation.2 | async-start | bytes 1179648 | tf_op jit(solution)/shard_map/all_gather | solution.py:69
Sparse Core Ops, SparseCore 0:
  49.0 47.8 all-gather.2
  104.7 37.0 all-gather.4

commit v2 on v0

v2 whole, which is shorter than its diff:
```python
import math

import jax
import jax.numpy as jnp
from jax import lax
from jax.experimental import pallas as pl
from jax.experimental.pallas import tpu as pltpu
from jax.sharding import PartitionSpec as P

MESH = pl.DeviceIdType.MESH
HALVES = 2
GROUP = 8
OFFSETS = ((1, 0), (3, 0), (0, 1), (1, 1), (3, 1), (2, 0), (2, 1))


def phases(base_band, band_count, earliest, count, interval):
    bands = base_band + jnp.arange(band_count, dtype=jnp.int32)
    times = earliest + jnp.arange(count, dtype=jnp.int32)
    return (bands[:, None] * times[None, :] % interval).astype(jnp.float32) * (
        2.0 * math.pi / interval
    )


def tables(base_band, band_count, earliest, count, interval):
    angles = phases(base_band, band_count, earliest, count, interval)
    both = jnp.stack([jnp.cos(angles), -jnp.sin(angles)], axis=1).reshape(2 * band_count, count)
    forward = (both * (1.0 / math.sqrt(interval))).astype(jnp.bfloat16)
    inverse = (both * (1.0 / math.sqrt(band_count))).astype(jnp.bfloat16)
    return forward, inverse.T


def spread(table, lanes):
    rows, inner = table.shape
    col = lax.broadcasted_iota(jnp.int32, (inner, lanes), 1) >> 3
    row = lax.broadcasted_iota(jnp.int32, (inner, lanes), 0)
    pick = jnp.where(col == row, 1.0, 0.0).astype(jnp.bfloat16)
    wide = jnp.dot(table, pick, preferred_element_type=jnp.float32)
    sub = lax.broadcasted_iota(jnp.int32, (1, GROUP, lanes), 1)
    lane = lax.broadcasted_iota(jnp.int32, (1, GROUP, lanes), 2) & (GROUP - 1)
    full = jnp.where(sub == lane, wide[:, None, :], 0.0)
    return full.reshape(rows * GROUP, lanes).astype(jnp.bfloat16)


def exchange_kernel(
    traces, reflection, forward, inverse, pieces, inv_out,
    samples, matrix, fwd_wide, inv_wide, partial, parts, spectra, acc, response,
    load_sem, mat_sem, inv_sem, own_sem,
    rs_send, rs_recv, ag_send, ag_recv, fw_send, core_recv, br_send, br_recv,
):
    f = lax.axis_index("freq")
    m = lax.axis_index("mat")
    x, yl = f // 2, f % 2
    z, yh, core = m // 4, (m // 2) % 2, m % 2

    def freq_peer(dx, dy):
        return lax.rem(x + dx, 4) * 2 + lax.rem(yl + dy, 2)

    def mat_peer(dz, dy):
        return lax.rem(z + dz, 4) * 4 + lax.rem(yh + dy, 2) * 2 + core

    other = m + 1 - 2 * core

    barrier = pltpu.get_barrier_semaphore()
    for o in OFFSETS:
        pl.semaphore_signal(barrier, inc=1, device_id=(freq_peer(*o), m), device_id_type=MESH)
        pl.semaphore_signal(barrier, inc=1, device_id=(f, mat_peer(*o)), device_id_type=MESH)
    pl.semaphore_signal(barrier, inc=1, device_id=(f, other), device_id_type=MESH)

    groups = samples.shape[0]
    per_half = groups // HALVES
    times = traces.shape[0]
    width = traces.shape[2]

    def load(g):
        return pltpu.make_async_copy(
            traces.at[:, pl.ds(pl.multiple_of(g * GROUP, GROUP), GROUP), :],
            samples.at[g],
            load_sem.at[g],
        )

    for g in range(groups):
        load(g).start()
    mat_load = pltpu.make_async_copy(reflection, matrix, mat_sem)
    mat_load.start()

    fwd_wide[...] = spread(forward[...], times * GROUP)

    def transform(h):
        def one(i, _):
            g = h * per_half + i
            load(g).wait()
            out = jnp.dot(
                fwd_wide[...],
                samples.at[g].reshape(times * GROUP, width)[...],
                preferred_element_type=jnp.float32,
            )
            out = out.reshape(8, 4, GROUP, width).astype(jnp.bfloat16)
            partial[h, :, :, i] = out
            return 0

        lax.fori_loop(0, per_half, one, 0)

    def rs_copy(h, j):
        to = freq_peer(*OFFSETS[j])
        return pltpu.make_async_remote_copy(
            src_ref=partial.at[h, to], dst_ref=parts.at[h, j],
            send_sem=rs_send.at[h, j], recv_sem=rs_recv.at[h, j],
            device_id=(to, m), device_id_type=MESH,
        )

    def ag_copy(h, j):
        return pltpu.make_async_remote_copy(
            src_ref=spectra.at[h, m], dst_ref=spectra.at[h, m],
            send_sem=ag_send.at[h, j], recv_sem=ag_recv.at[h, j],
            device_id=(f, mat_peer(*OFFSETS[j])), device_id_type=MESH,
        )

    def core_copy(h, j, block):
        return pltpu.make_async_remote_copy(
            src_ref=spectra.at[h, block], dst_ref=spectra.at[h, block],
            send_sem=fw_send.at[h, j], recv_sem=core_recv.at[h, j],
            device_id=(f, other), device_id_type=MESH,
        )

    def br_copy(h, j):
        return pltpu.make_async_remote_copy(
            src_ref=response.at[h], dst_ref=pieces.at[h, f],
            send_sem=br_send.at[h, j], recv_sem=br_recv.at[h, j],
            device_id=(freq_peer(*OFFSETS[j]), m), device_id_type=MESH,
        )

    peers = range(len(OFFSETS))
    last = len(OFFSETS)

    for h in range(HALVES):
        transform(h)
        if h == 0:
            pl.semaphore_wait(barrier, 2 * len(OFFSETS) + 1)
        for j in peers:
            rs_copy(h, j).start()

    inv_wide[...] = spread(inverse[...], inv_wide.shape[1])
    inv_copy = pltpu.make_async_copy(inv_wide, inv_out, inv_sem)
    inv_copy.start()

    for h in range(HALVES):
        total = partial[h, f].astype(jnp.float32)
        for j in peers:
            rs_copy(h, j).wait_recv()
            total = total + parts[h, j].astype(jnp.float32)
        spectra[h, m] = total.astype(jnp.bfloat16)
        for j in peers:
            ag_copy(h, j).start()
        core_copy(h, last, m).start()

    mat_load.wait()
    bands = matrix.shape[0]
    half_rows = per_half * GROUP
    recv_rows = matrix.shape[2]

    def multiply(h, block, first):
        for k in range(bands):
            panel = spectra.at[h, block, pl.ds(2 * k, 2)].reshape(2 * half_rows, width)[...]
            cols = pl.ds(pl.multiple_of(block * width, width), width)
            tile = matrix[k, :, :, cols].reshape(2 * recv_rows, width)
            out = lax.dot_general(
                panel, tile, (((1,), (1,)), ((), ())), preferred_element_type=jnp.float32
            )
            if first:
                acc[k] = out
            else:
                acc[k] += out

    for h in range(HALVES):
        multiply(h, m, True)
        core_copy(h, last, m).wait_recv()
        multiply(h, other, False)
        for j in peers:
            block = mat_peer(*OFFSETS[j])
            ag_copy(h, j).wait_recv()
            core_copy(h, j, source(h, j, mat_peer)).start()
            multiply(h, source(h, j, mat_peer), False)
            core_copy(h, j, m).wait_recv()
            multiply(h, source(h, j, mat_peer) + 1 - 2 * core, False)
        for k in range(bands):
            a = acc[k]
            real = a[:half_rows, :recv_rows] - a[half_rows:, recv_rows:]
            imag = a[half_rows:, :recv_rows] + a[:half_rows, recv_rows:]
            response[h, 2 * k] = real.reshape(per_half, GROUP, width).astype(jnp.bfloat16)
            response[h, 2 * k + 1] = imag.reshape(per_half, GROUP, width).astype(jnp.bfloat16)
        for j in peers:
            br_copy(h, j).start()
        pltpu.make_async_copy(response.at[h], pieces.at[h, f], own_sem.at[h]).start()

    for h in range(HALVES):
        for j in peers:
            br_copy(h, j).wait_recv()
        pltpu.make_async_copy(response.at[h], pieces.at[h, f], own_sem.at[h]).wait()
    for h in range(HALVES):
        for j in peers:
            rs_copy(h, j).wait_send()
            ag_copy(h, j).wait_send()
            core_copy(h, j, m).wait_send()
            br_copy(h, j).wait_send()
        core_copy(h, last, m).wait_send()
    inv_copy.wait()


def source(h, j, mat_peer):
    dz, dy = OFFSETS[j]
    return mat_peer((4 - dz) % 4, dy)


def window_kernel(table, pieces, onset, out):
    times = out.shape[0]
    width = out.shape[2]
    step = 32
    rows = pieces[...].astype(jnp.float32).reshape(table.shape[1], width).astype(jnp.bfloat16)
    left = onset[...] - lax.axis_index("freq") * times
    at = lax.broadcasted_iota(jnp.int32, (step, GROUP, width), 0)

    def one(i, _):
        t = pl.multiple_of(i * step, step)
        signal = jnp.dot(
            table[pl.ds(pl.multiple_of(i * step * GROUP, step * GROUP), step * GROUP), :],
            rows,
            preferred_element_type=jnp.float32,
        ).reshape(step, GROUP, width)
        kept = jnp.where(at < (left - t)[None], signal, 0.0)
        out[pl.ds(t, step)] = kept.astype(jnp.bfloat16)
        return 0

    lax.fori_loop(0, times // step, one, 0, unroll=2)


def on_device(traces, reflection, onset):
    times, focal, width = traces.shape
    devices = lax.axis_size("freq")
    mats = lax.axis_size("mat")
    interval = times * devices
    per_device = reflection.shape[0]
    bands = per_device * devices
    rows = 2 * per_device
    half = focal // HALVES
    per_half = half // GROUP
    peers = len(OFFSETS)
    forward, inverse = tables(
        interval // 16, bands, lax.axis_index("freq") * times, times, interval
    )
    bf16 = jnp.bfloat16
    dma = pltpu.SemaphoreType.DMA
    anywhere = pl.BlockSpec(memory_space=pl.ANY)
    vmem = pl.BlockSpec(memory_space=pltpu.VMEM)
    pieces, table = pl.pallas_call(
        exchange_kernel,
        out_shape=(
            jax.ShapeDtypeStruct((HALVES, devices, rows, per_half, GROUP, width), bf16),
            jax.ShapeDtypeStruct((times * GROUP, 2 * bands * GROUP), bf16),
        ),
        in_specs=[anywhere, anywhere, vmem, vmem],
        out_specs=(anywhere, anywhere),
        scratch_shapes=[
            pltpu.VMEM((focal // GROUP, times, GROUP, width), bf16),
            pltpu.VMEM(reflection.shape, bf16),
            pltpu.VMEM((2 * bands * GROUP, times * GROUP), bf16),
            pltpu.VMEM((times * GROUP, 2 * bands * GROUP), bf16),
            pltpu.VMEM((HALVES, devices, rows, per_half, GROUP, width), bf16),
            pltpu.VMEM((HALVES, peers, rows, per_half, GROUP, width), bf16),
            pltpu.VMEM((HALVES, mats, rows, per_half, GROUP, width), bf16),
            pltpu.VMEM((per_device, 2 * half, 2 * width), jnp.float32),
            pltpu.VMEM((HALVES, rows, per_half, GROUP, width), bf16),
            dma((focal // GROUP,)),
            dma,
            dma,
            dma((HALVES,)),
            dma((HALVES, peers)),
            dma((HALVES, peers)),
            dma((HALVES, peers)),
            dma((HALVES, peers)),
            dma((HALVES, peers + 1)),
            dma((HALVES, peers + 1)),
            dma((HALVES, peers)),
            dma((HALVES, peers)),
        ],
        compiler_params=pltpu.CompilerParams(
            collective_id=0, has_side_effects=True, vmem_limit_bytes=60 * 2**20
        ),
        name="exchange",
    )(traces, reflection, forward, inverse)
    return pl.pallas_call(
        window_kernel,
        grid=(focal // GROUP,),
        out_shape=jax.ShapeDtypeStruct((times, focal, width), bf16),
        in_specs=[
            pl.BlockSpec(table.shape, lambda g: (0, 0)),
            pl.BlockSpec(
                (None, devices, rows, None, GROUP, width),
                lambda g: (g // per_half, 0, 0, g % per_half, 0, 0),
            ),
            pl.BlockSpec((GROUP, width), lambda g: (g, 0)),
        ],
        out_specs=pl.BlockSpec((times, GROUP, width), lambda g: (0, g, 0)),
        compiler_params=pltpu.CompilerParams(vmem_limit_bytes=60 * 2**20),
        name="window",
    )(table, pieces, onset)


def solution(mesh):
    placed = (P("freq", None, "mat"), P("freq", None, "mat", None), P(None, "mat"))
    return jax.shard_map(
        on_device, mesh=mesh, in_specs=placed, out_specs=P("freq", None, "mat"), check_vma=False
    )
```

time: 295 us -> 63.4 us (0.21); the launches traced: 290 us -> 63.1 us
  waiting for transfers between devices: 197 us -> 0 us
  Pallas kernels: 0 us -> 61.5 us
  local copies, waits for them, and re-layouts: 47.5 us -> 1.39 us
  matrix products: 16.5 us -> 0 us
  between operations: 13.5 us -> 0.04 us
  blocking collectives: 8.09 us -> 0 us
  starting transfers between devices: 6.34 us -> 0 us
    all_to_all x1 -> x0, waiting for transfers between devices: 114 us -> none  [on_device(): lax.all_to_all(traces, 'freq', split_axis=1, concat_axis=0, tiled=True)]
    all_gather x2 -> x0, waiting for transfers between devices: 82.8 us -> none  [the longest x1 50.8 us: on_device(): lax.all_gather(spectra, 'mat', axis=3, tiled=True)]
    pallas_call x0 -> x2, Pallas kernels: none -> 61.5 us  [the longest x1 51.2 us: on_device(): pl.pallas_call(exchange_kernel, out_shape=(jax.ShapeDtypeStruct((HALVES,...]
    unnamed x5 -> x0, local copies, waits for them, and re-layouts: 21.9 us -> none
    dot_general x3 -> x0, matrix products: 16.5 us -> none  [the longest x1 6.94 us: accumulate(): jnp.einsum('kcpw,kdrw->kcpdr', panels, reflection, preferred_element_type...]
    all_to_all x2 -> x0, local copies, waits for them, and re-layouts: 12.6 us -> none  [the longest x1 11.9 us: on_device(): lax.all_to_all(traces, 'freq', split_axis=1, concat_axis=0, tiled=True)]
    convert_element_type x3 -> x5, local copies, waits for them, and re-layouts: 11.6 us -> 1.39 us  [the longest x3 0.76 us: tables(): inverse = (both * (1.0 / math.sqrt(band_count))).astype(jnp.bfloat16)]
    all_to_all x1 -> x0, blocking collectives: 8.09 us -> none  [on_device(): lax.all_to_all(local_spectra, 'freq', split_axis=0, concat_axis=2, tiled=...]
  transfers between devices with their start and end apart: 3 -> 0, of which waited for: 3 -> 0; matrix products, arithmetic and copies ran while one was open for 0% -> 0% of each run, Pallas kernels for 0% -> 0%
where the time goes in v2:
time: 63.4 us; the launch traced here: 63.1 us
  Pallas kernels  61.5 us (97%)
  local copies, waits for them, and re-layouts  1.39 us (2%)
    pallas_call x1, Pallas kernels, on_device(): pl.pallas_call(exchange_kernel, out_shape=(jax.ShapeDtypeStruct((HALVES,...  51.2 us
    pallas_call x1, Pallas kernels, on_device(): pl.pallas_call(window_kernel, grid=(focal // GROUP,), out_shape=jax.Shape...  10.3 us

profile of v2, /device:TPU:1, one launch (start us, length us, event | category | flops | bytes accessed | tf_op | source)
XLA Modules:
  0.0 63.1 jit_solution(18264482442098387199)
XLA Ops:
  0.0 0.2 fusion.3
  0.2 0.6 convert_element_type.27.forward
  0.9 0.7 %copy.8 = bf16[32,256]{0,1:T(8,128)(2,1)} copy(bf16[32,256]{1,0:T(8,128)(2,1)S(1)} %convert_element_type.29) | data formatting | bytes 32768 | tf_op jit(solution)/shard_map/convert_element_type | solution.py:28
  1.6 51.2 %exchange.1 = (bf16[2,8,4,4,8,256]{5,4,3,2,1,0:T(8,128)(2,1)}, bf16[2048,256]{1,0:T(8,128)(2,1)}) custom-call(bf16[256,64,256]{2,1,0:T(8,128)(2,1)} %traces.1, bf16[2,2,256,4096]{3,2,1,0:T(8,128)(2,1)} %reflection.1, bf16[32,256]{1,0:T(8,128)(2,1)} %convert_element_type.27.forward, bf16[256,32]{1,0:T(8,128)(2,1)} %bitcast.1), custom_call_target="tpu_custom_call" | custom-call | tf_op jit(solution)/shard_map/exchange/pallas_call | solution.py:254
  52.8 10.3 %window.1 = bf16[256,64,256]{2,1,0:T(8,128)(2,1)} custom-call(bf16[2048,256]{1,0:T(8,128)(2,1)} %get-tuple-element.7.table, bf16[2,8,4,4,8,256]{5,4,3,2,1,0:T(8,128)(2,1)} %get-tuple-element.8.pieces, s32[64,256]{1,0:T(8,128)} %onset.1), custom_call_target="tpu_custom_call" | custom-call | tf_op jit(solution)/shard_map/window/pallas_call | solution.py:290
  (6 shorter events, 0.1 us)

commit v3 on v2

v3 whole, which is shorter than its diff:
```python
import math

import jax
import jax.numpy as jnp
from jax import lax
from jax.experimental import pallas as pl
from jax.experimental.pallas import tpu as pltpu
from jax.sharding import PartitionSpec as P

MESH = pl.DeviceIdType.MESH
HALVES = 4
GROUP = 8
STEPS = 4
LEAD, SPACING = (-6.0, 0.0, 3.8, 5.0, 8.0), 9.6
OFFSETS = ((0, 1), (1, 0), (3, 0), (2, 0), (1, 1), (3, 1), (2, 1))
ACROSS, DIRECT, RELAYED = 0, (0, 1, 2, 3), (4, 5, 6)


def table_pair(first, bands, times, interval):
    k = first + lax.broadcasted_iota(jnp.int32, (bands, times), 0)
    t = lax.axis_index("freq") * times + lax.broadcasted_iota(jnp.int32, (bands, times), 1)
    angles = ((k * t) & (interval - 1)).astype(jnp.float32) * (2.0 * math.pi / interval)
    return jnp.cos(angles), -jnp.sin(angles)


def kron_rows(wide):
    rows, lanes = wide.shape
    sub = lax.broadcasted_iota(jnp.int32, (1, GROUP, lanes), 1)
    lane = lax.broadcasted_iota(jnp.int32, (1, GROUP, lanes), 2) & (GROUP - 1)
    full = jnp.where(sub == lane, wide[:, None, :], 0.0)
    return full.reshape(rows * GROUP, lanes).astype(jnp.bfloat16)


def repeat_lanes(inner, lanes):
    col = lax.broadcasted_iota(jnp.int32, (inner, lanes), 1) >> 3
    row = lax.broadcasted_iota(jnp.int32, (inner, lanes), 0)
    return jnp.where(col == row, 1.0, 0.0).astype(jnp.bfloat16)


def exchange_kernel(
    traces, reflection, pieces, inv_out,
    samples, matrix, fwd_wide, inv_wide, partial, parts, spectra, acc, response,
    load_sem, mat_sem, inv_sem, own_sem,
    rs_send, rs_recv, ag_send, ag_recv, fw_send, core_recv, br_send, br_recv,
):
    f = lax.axis_index("freq")
    m = lax.axis_index("mat")
    x, yl = f // 2, f % 2
    z, yh, core = m // 4, (m // 2) % 2, m % 2

    def freq_peer(dx, dy):
        return lax.rem(x + dx, 4) * 2 + lax.rem(yl + dy, 2)

    def mat_peer(dz, dy):
        return lax.rem(z + dz, 4) * 4 + lax.rem(yh + dy, 2) * 2 + core

    def source(j):
        dz, dy = OFFSETS[j]
        return mat_peer((4 - dz) % 4, dy)

    flip = 1 - 2 * core
    other = m + flip
    freq_ids = [freq_peer(*o) for o in OFFSETS]
    mat_ids = [mat_peer(*o) for o in OFFSETS]

    barrier = pltpu.get_barrier_semaphore()
    for o in OFFSETS:
        pl.semaphore_signal(barrier, inc=1, device_id=(freq_peer(*o), m), device_id_type=MESH)
        pl.semaphore_signal(barrier, inc=1, device_id=(f, mat_peer(*o)), device_id_type=MESH)
    pl.semaphore_signal(barrier, inc=1, device_id=(f, other), device_id_type=MESH)

    groups = samples.shape[0]
    per_half = groups // HALVES
    times = traces.shape[0]
    width = traces.shape[2]

    def load(g):
        return pltpu.make_async_copy(
            traces.at[:, pl.ds(pl.multiple_of(g * GROUP, GROUP), GROUP), :],
            samples.at[g],
            load_sem.at[g],
        )

    for g in range(groups):
        load(g).start()
    mat_load = pltpu.make_async_copy(reflection, matrix, mat_sem)

    bands_here = matrix.shape[0]
    owners = partial.shape[1]
    bands = bands_here * owners
    interval = times * owners
    table = jnp.concatenate(table_pair(interval // 16, bands, times, interval), axis=0)
    forward = (table * (1.0 / math.sqrt(interval))).astype(jnp.bfloat16)
    fwd_wide[...] = kron_rows(
        jnp.dot(
            forward, repeat_lanes(times, times * GROUP), preferred_element_type=jnp.float32
        )
    )

    def transform(h):
        def one(i, _):
            g = h * per_half + i
            load(g).wait()
            out = jnp.dot(
                fwd_wide[...],
                samples.at[g].reshape(times * GROUP, width)[...],
                preferred_element_type=jnp.float32,
            )
            out = out.reshape(2, owners, bands_here, GROUP, width).astype(jnp.bfloat16)
            partial[h, :, :, 0, i] = out[0]
            partial[h, :, :, 1, i] = out[1]
            return 0

        lax.fori_loop(0, per_half, one, 0)

    def rs_copy(h, j):
        to = freq_ids[j]
        return pltpu.make_async_remote_copy(
            src_ref=partial.at[h, to], dst_ref=parts.at[h, j],
            send_sem=rs_send.at[h], recv_sem=rs_recv.at[h],
            device_id=(to, m), device_id_type=MESH,
        )

    def rs_all(h):
        return pltpu.make_async_remote_copy(
            src_ref=parts.at[h], dst_ref=parts.at[h],
            send_sem=rs_send.at[h], recv_sem=rs_recv.at[h],
            device_id=(f, other), device_id_type=MESH,
        )

    def ag_copy(h, j):
        relayed = j in RELAYED
        kind = 2 if relayed else int(j != ACROSS)
        return pltpu.make_async_remote_copy(
            src_ref=spectra.at[h, core, (1 + ACROSS) if relayed else 0],
            dst_ref=spectra.at[h, core, 1 + j],
            send_sem=ag_send.at[h, kind], recv_sem=ag_recv.at[h, kind],
            device_id=(f, mat_ids[j - 3] if relayed else mat_ids[j]), device_id_type=MESH,
        )

    def ag_all(h, kind):
        first, count = ((1, 1), (2, 3), (5, 3))[kind]
        part = spectra.at[h, core, pl.ds(first, count)]
        return pltpu.make_async_remote_copy(
            src_ref=part, dst_ref=part,
            send_sem=ag_send.at[h, kind], recv_sem=ag_recv.at[h, kind],
            device_id=(f, other), device_id_type=MESH,
        )

    def core_copy(h, part):
        first, count = ((0, 5), (5, 3))[part]
        held = spectra.at[h, core, pl.ds(first, count)]
        return pltpu.make_async_remote_copy(
            src_ref=held, dst_ref=held,
            send_sem=fw_send.at[h, part], recv_sem=core_recv.at[h, part],
            device_id=(f, other), device_id_type=MESH,
        )

    def br_copy(h, j):
        return pltpu.make_async_remote_copy(
            src_ref=response.at[h], dst_ref=pieces.at[h, f],
            send_sem=br_send.at[h], recv_sem=br_recv.at[h],
            device_id=(freq_ids[j], m), device_id_type=MESH,
        )

    def br_all(h):
        part = pieces.at[h, pl.ds(0, len(OFFSETS))]
        return pltpu.make_async_remote_copy(
            src_ref=part, dst_ref=part,
            send_sem=br_send.at[h], recv_sem=br_recv.at[h],
            device_id=(f, other), device_id_type=MESH,
        )

    peers = range(len(OFFSETS))

    for h in range(HALVES):
        transform(h)
        if h == 0:
            mat_load.start()
            pl.semaphore_wait(barrier, 2 * len(OFFSETS) + 1)
            for j in peers:
                rs_copy(h, j).start()

    inverse = (table * (1.0 / math.sqrt(bands))).astype(jnp.bfloat16)
    inv_wide[...] = kron_rows(
        lax.dot_general(
            inverse,
            repeat_lanes(2 * bands, 2 * bands * GROUP),
            (((0,), (0,)), ((), ())),
            preferred_element_type=jnp.float32,
        )
    )
    inv_copy = pltpu.make_async_copy(inv_wide, inv_out, inv_sem)
    inv_copy.start()

    half_rows = per_half * GROUP
    recv_rows = matrix.shape[2]

    def multiply(h, side, slot):
        block = m if slot == 0 else source(slot - 1)
        block = block + (side - core)
        for k in range(bands_here):
            panel = spectra.at[h, side, slot, k].reshape(2 * half_rows, width)[...]
            cols = pl.ds(pl.multiple_of(block * width, width), width)
            tile = matrix[k, :, :, cols].reshape(2 * recv_rows, width)
            out = lax.dot_general(
                panel, tile, (((1,), (1,)), ((), ())), preferred_element_type=jnp.float32
            )
            if slot == 0 and side is core:
                acc[h, k] = out
            else:
                acc[h, k] += out

    def send_parts(h):
        if h == 0:
            return
        rs_all(h - 1).wait_send()
        for j in peers:
            rs_copy(h, j).start()

    def add_up(h):
        rs_all(h).wait_recv()
        total = partial[h, f].astype(jnp.float32)
        for j in peers:
            total = total + parts[h, j].astype(jnp.float32)
        spectra[h, core, 0] = total.astype(jnp.bfloat16)
        for j in DIRECT:
            ag_copy(h, j).start()

    def relay(h):
        ag_all(h, 0).wait_recv()
        for j in RELAYED:
            ag_copy(h, j).start()

    def first_blocks(h):
        if h == 0:
            mat_load.wait()
        ag_all(h, 1).wait_recv()
        core_copy(h, 0).start()
        for slot in range(5):
            multiply(h, core, slot)

    def last_blocks(h):
        ag_all(h, 2).wait_recv()
        core_copy(h, 1).start()
        for slot in range(5, 8):
            multiply(h, core, slot)
        core_copy(h, 0).wait_recv()
        for slot in range(5):
            multiply(h, 1 - core, slot)
        core_copy(h, 1).wait_recv()
        for slot in range(5, 8):
            multiply(h, 1 - core, slot)
        for k in range(bands_here):
            a = acc[h, k]
            real = a[:half_rows, :recv_rows] - a[half_rows:, recv_rows:]
            imag = a[half_rows:, :recv_rows] + a[:half_rows, recv_rows:]
            response[h, k, 0] = real.reshape(per_half, GROUP, width).astype(jnp.bfloat16)
            response[h, k, 1] = imag.reshape(per_half, GROUP, width).astype(jnp.bfloat16)
        for j in peers:
            br_copy(h, j).start()
        pltpu.make_async_copy(response.at[h], pieces.at[h, f], own_sem.at[h]).start()

    steps = (send_parts, add_up, relay, first_blocks, last_blocks)
    order = sorted(
        (LEAD[i] + h * SPACING / HALVES, i, h) for i in range(len(steps)) for h in range(HALVES)
    )
    for _, i, h in order:
        steps[i](h)

    for h in range(HALVES):
        br_all(h).wait_recv()
        pltpu.make_async_copy(response.at[h], pieces.at[h, f], own_sem.at[h]).wait()
    rs_all(HALVES - 1).wait_send()
    for h in range(HALVES):
        for kind in range(3):
            ag_all(h, kind).wait_send()
        for part in range(2):
            core_copy(h, part).wait_send()
        br_all(h).wait_send()
    inv_copy.wait()


def window_kernel(table, pieces, onset, out, wide, held, left, rows, signal, sems, tab_sem, out_sem):
    times, focal, width = out.shape
    steps = signal.shape[0]
    step = times // steps
    groups = focal // GROUP

    def table_load(i):
        part = pl.ds(i * step * GROUP, step * GROUP)
        return pltpu.make_async_copy(table.at[part], wide.at[part], tab_sem.at[i])

    def store(i):
        return pltpu.make_async_copy(
            signal.at[i], out.at[pl.ds(i * step, step)], out_sem.at[i]
        )

    loads = [pltpu.make_async_copy(pieces.at[h], held.at[h], sems.at[h]) for h in range(HALVES)]
    loads.append(pltpu.make_async_copy(onset, left, sems.at[HALVES]))
    for copy in loads:
        copy.start()
    for i in range(steps):
        table_load(i).start()
    for copy in loads:
        copy.wait()
    per_half = groups // HALVES
    for g in range(groups):
        parts = [
            held[g // per_half, :, :, c, g % per_half]
            .astype(jnp.float32)
            .reshape(wide.shape[1] // 2, width)
            for c in range(2)
        ]
        rows[g] = jnp.concatenate(parts, axis=0).astype(jnp.bfloat16)
    at = lax.axis_index("freq") * times + lax.broadcasted_iota(
        jnp.int32, (step, GROUP, width), 0
    )
    for i in range(steps):
        table_load(i).wait()
        weights = wide[i * step * GROUP : (i + 1) * step * GROUP]
        for g in range(groups):
            value = jnp.dot(weights, rows[g], preferred_element_type=jnp.float32)
            until = left[g * GROUP : (g + 1) * GROUP] - i * step
            kept = jnp.where(at < until[None], value.reshape(step, GROUP, width), 0.0)
            signal[i, :, g * GROUP : (g + 1) * GROUP] = kept.astype(jnp.bfloat16)
        store(i).start()
    for i in range(steps):
        store(i).wait()


def on_device(traces, reflection, onset):
    times, focal, width = traces.shape
    devices = lax.axis_size("freq")
    mats = lax.axis_size("mat")
    per_device = reflection.shape[0]
    bands = per_device * devices
    half = focal // HALVES
    per_half = half // GROUP
    peers = len(OFFSETS)
    bf16 = jnp.bfloat16
    dma = pltpu.SemaphoreType.DMA
    anywhere = pl.BlockSpec(memory_space=pl.ANY)
    pieces, table = pl.pallas_call(
        exchange_kernel,
        out_shape=(
            jax.ShapeDtypeStruct((HALVES, devices, per_device, 2, per_half, GROUP, width), bf16),
            jax.ShapeDtypeStruct((times * GROUP, 2 * bands * GROUP), bf16),
        ),
        in_specs=[anywhere, anywhere],
        out_specs=(anywhere, anywhere),
        scratch_shapes=[
            pltpu.VMEM((focal // GROUP, times, GROUP, width), bf16),
            pltpu.VMEM(reflection.shape, bf16),
            pltpu.VMEM((2 * bands * GROUP, times * GROUP), bf16),
            pltpu.VMEM((times * GROUP, 2 * bands * GROUP), bf16),
            pltpu.VMEM((HALVES, devices, per_device, 2, per_half, GROUP, width), bf16),
            pltpu.VMEM((HALVES, peers, per_device, 2, per_half, GROUP, width), bf16),
            pltpu.VMEM((HALVES, 2, mats // 2, per_device, 2, per_half, GROUP, width), bf16),
            pltpu.VMEM((HALVES, per_device, 2 * half, 2 * width), jnp.float32),
            pltpu.VMEM((HALVES, per_device, 2, per_half, GROUP, width), bf16),
            dma((focal // GROUP,)),
            dma,
            dma,
            dma((HALVES,)),
            dma((HALVES,)),
            dma((HALVES,)),
            dma((HALVES, 3)),
            dma((HALVES, 3)),
            dma((HALVES, 2)),
            dma((HALVES, 2)),
            dma((HALVES,)),
            dma((HALVES,)),
        ],
        compiler_params=pltpu.CompilerParams(
            collective_id=0, has_side_effects=True, vmem_limit_bytes=60 * 2**20
        ),
        name="exchange",
    )(traces, reflection)
    return pl.pallas_call(
        window_kernel,
        out_shape=jax.ShapeDtypeStruct((times, focal, width), bf16),
        in_specs=[anywhere, anywhere, anywhere],
        out_specs=anywhere,
        scratch_shapes=[
            pltpu.VMEM(table.shape, bf16),
            pltpu.VMEM(pieces.shape, bf16),
            pltpu.VMEM(onset.shape, jnp.int32),
            pltpu.VMEM((focal // GROUP, table.shape[1], width), bf16),
            pltpu.VMEM((STEPS, times // STEPS, focal, width), bf16),
            dma((HALVES + 1,)),
            dma((STEPS,)),
            dma((STEPS,)),
        ],
        compiler_params=pltpu.CompilerParams(vmem_limit_bytes=60 * 2**20),
        name="window",
    )(table, pieces, onset)


def solution(mesh):
    placed = (P("freq", None, "mat"), P("freq", None, "mat", None), P(None, "mat"))
    return jax.shard_map(
        on_device, mesh=mesh, in_specs=placed, out_specs=P("freq", None, "mat"), check_vma=False
    )
```

time: 63.4 us -> 49.4 us (0.78)
  Pallas kernels: 61.5 us -> 49.2 us
  local copies, waits for them, and re-layouts: 1.39 us -> 0 us
    pallas_call x1, Pallas kernels: 51.2 us -> 43.5 us  [on_device(): pl.pallas_call(exchange_kernel, out_shape=(jax.ShapeDtypeStruct((HALVES,...]
    pallas_call x1, Pallas kernels: 10.3 us -> 5.77 us  [on_device(): pl.pallas_call(window_kernel, out_shape=jax.ShapeDtypeStruct((times, foca...]
    convert_element_type x5 -> x0, local copies, waits for them, and re-layouts: 1.39 us -> none  [the longest x3 0.76 us: tables(): inverse = (both * (1.0 / math.sqrt(band_count))).astype(jnp.bfloat16)]
where the time goes in v3:
time: 49.4 us; the launch traced here: 49.2 us
  Pallas kernels  49.2 us (100%)
    pallas_call x1, Pallas kernels, on_device(): pl.pallas_call(exchange_kernel, out_shape=(jax.ShapeDtypeStruct((HALVES,...  43.5 us
    pallas_call x1, Pallas kernels, on_device(): pl.pallas_call(window_kernel, out_shape=jax.ShapeDtypeStruct((times, foca...  5.77 us

profile of v3, /device:TPU:1, one launch (start us, length us, event | category | flops | bytes accessed | tf_op | source)
XLA Modules:
  0.0 49.2 jit_solution(1811659979922703010)
XLA Ops:
  0.0 43.5 %exchange.1 = (bf16[4,8,2,2,2,8,256]{6,5,4,3,2,1,0:T(8,128)(2,1)}, bf16[2048,256]{1,0:T(8,128)(2,1)}) custom-call(bf16[256,64,256]{2,1,0:T(8,128)(2,1)} %traces.1, bf16[2,2,256,4096]{3,2,1,0:T(8,128)(2,1)} %reflection.1), custom_call_target="tpu_custom_call" | custom-call | tf_op jit(solution)/shard_map/exchange/pallas_call | solution.py:344
  43.5 5.8 %window.1 = bf16[256,64,256]{2,1,0:T(8,128)(2,1)} custom-call(bf16[2048,256]{1,0:T(8,128)(2,1)} %get-tuple-element.7.table, bf16[4,8,2,2,2,8,256]{6,5,4,3,2,1,0:T(8,128)(2,1)} %get-tuple-element.8.pieces, s32[64,256]{1,0:T(8,128)} %onset.1), custom_call_target="tpu_custom_call" | custom-call | tf_op jit(solution)/shard_map/window/pallas_call | solution.py:380

commit v4 on v3

--- a/solution.py
+++ b/solution.py
@@ -11,7 +11,7 @@
 HALVES = 4
 GROUP = 8
 STEPS = 4
-LEAD, SPACING = (-6.0, 0.0, 3.8, 5.0, 8.0), 9.6
+LEAD, SPACING = (-4.5, 0.0, 3.8, 5.0, 8.0), 9.6
 OFFSETS = ((0, 1), (1, 0), (3, 0), (2, 0), (1, 1), (3, 1), (2, 1))
 ACROSS, DIRECT, RELAYED = 0, (0, 1, 2, 3), (4, 5, 6)
 

time: 49.4 us -> 46.8 us (0.947)
  Pallas kernels: 49.2 us -> 46.7 us
    pallas_call x1, Pallas kernels: 43.5 us -> 40.9 us  [on_device(): pl.pallas_call(exchange_kernel, out_shape=(jax.ShapeDtypeStruct((HALVES,...]
where the time goes in v4:
time: 46.8 us; the launch traced here: 46.7 us
  Pallas kernels  46.7 us (100%)
    pallas_call x1, Pallas kernels, on_device(): pl.pallas_call(exchange_kernel, out_shape=(jax.ShapeDtypeStruct((HALVES,...  40.9 us
    pallas_call x1, Pallas kernels, on_device(): pl.pallas_call(window_kernel, out_shape=jax.ShapeDtypeStruct((times, foca...  5.77 us

profile of v4, /device:TPU:1, one launch (start us, length us, event | category | flops | bytes accessed | tf_op | source)
XLA Modules:
  0.0 46.7 jit_solution(3230861342351523875)
XLA Ops:
  0.0 40.9 %exchange.1 = (bf16[4,8,2,2,2,8,256]{6,5,4,3,2,1,0:T(8,128)(2,1)}, bf16[2048,256]{1,0:T(8,128)(2,1)}) custom-call(bf16[256,64,256]{2,1,0:T(8,128)(2,1)} %traces.1, bf16[2,2,256,4096]{3,2,1,0:T(8,128)(2,1)} %reflection.1), custom_call_target="tpu_custom_call" | custom-call | tf_op jit(solution)/shard_map/exchange/pallas_call | solution.py:344
  40.9 5.8 %window.1 = bf16[256,64,256]{2,1,0:T(8,128)(2,1)} custom-call(bf16[2048,256]{1,0:T(8,128)(2,1)} %get-tuple-element.7.table, bf16[4,8,2,2,2,8,256]{6,5,4,3,2,1,0:T(8,128)(2,1)} %get-tuple-element.8.pieces, s32[64,256]{1,0:T(8,128)} %onset.1), custom_call_target="tpu_custom_call" | custom-call | tf_op jit(solution)/shard_map/window/pallas_call | solution.py:380

commit v5 on v4

--- a/solution.py
+++ b/solution.py
@@ -13,6 +13,7 @@
 STEPS = 4
 LEAD, SPACING = (-4.5, 0.0, 3.8, 5.0, 8.0), 9.6
 OFFSETS = ((0, 1), (1, 0), (3, 0), (2, 0), (1, 1), (3, 1), (2, 1))
+FREQ_OFFSETS = ((0, 1), (1, 1), (3, 1), (2, 1), (1, 0), (3, 0), (2, 0))
 ACROSS, DIRECT, RELAYED = 0, (0, 1, 2, 3), (4, 5, 6)
 
 
@@ -60,7 +61,7 @@
 
     flip = 1 - 2 * core
     other = m + flip
-    freq_ids = [freq_peer(*o) for o in OFFSETS]
+    freq_ids = [freq_peer(*o) for o in FREQ_OFFSETS]
     mat_ids = [mat_peer(*o) for o in OFFSETS]
 
     barrier = pltpu.get_barrier_semaphore()
@@ -257,6 +258,8 @@
             imag = a[half_rows:, :recv_rows] + a[:half_rows, recv_rows:]
             response[h, k, 0] = real.reshape(per_half, GROUP, width).astype(jnp.bfloat16)
             response[h, k, 1] = imag.reshape(per_half, GROUP, width).astype(jnp.bfloat16)
+        if h:
+            br_all(h - 1).wait_send()
         for j in peers:
             br_copy(h, j).start()
         pltpu.make_async_copy(response.at[h], pieces.at[h, f], own_sem.at[h]).start()
@@ -277,7 +280,7 @@
             ag_all(h, kind).wait_send()
         for part in range(2):
             core_copy(h, part).wait_send()
-        br_all(h).wait_send()
+    br_all(HALVES - 1).wait_send()
     inv_copy.wait()
 
 

time: 46.8 us -> 46.1 us (0.985)
  Pallas kernels: 46.7 us -> 45.9 us
    pallas_call x1, Pallas kernels: 40.9 us -> 40.2 us  [on_device(): pl.pallas_call(exchange_kernel, out_shape=(jax.ShapeDtypeStruct((HALVES,...]
where the time goes in v5:
time: 46.1 us; the launch traced here: 45.9 us
  Pallas kernels  45.9 us (100%)
    pallas_call x1, Pallas kernels, on_device(): pl.pallas_call(exchange_kernel, out_shape=(jax.ShapeDtypeStruct((HALVES,...  40.2 us
    pallas_call x1, Pallas kernels, on_device(): pl.pallas_call(window_kernel, out_shape=jax.ShapeDtypeStruct((times, foca...  5.77 us

profile of v5, /device:TPU:1, one launch (start us, length us, event | category | flops | bytes accessed | tf_op | source)
XLA Modules:
  0.0 45.9 jit_solution(14398016112481355908)
XLA Ops:
  0.0 40.2 %exchange.1 = (bf16[4,8,2,2,2,8,256]{6,5,4,3,2,1,0:T(8,128)(2,1)}, bf16[2048,256]{1,0:T(8,128)(2,1)}) custom-call(bf16[256,64,256]{2,1,0:T(8,128)(2,1)} %traces.1, bf16[2,2,256,4096]{3,2,1,0:T(8,128)(2,1)} %reflection.1), custom_call_target="tpu_custom_call" | custom-call | tf_op jit(solution)/shard_map/exchange/pallas_call | solution.py:347
  40.2 5.8 %window.1 = bf16[256,64,256]{2,1,0:T(8,128)(2,1)} custom-call(bf16[2048,256]{1,0:T(8,128)(2,1)} %get-tuple-element.7.table, bf16[4,8,2,2,2,8,256]{6,5,4,3,2,1,0:T(8,128)(2,1)} %get-tuple-element.8.pieces, s32[64,256]{1,0:T(8,128)} %onset.1), custom_call_target="tpu_custom_call" | custom-call | tf_op jit(solution)/shard_map/window/pallas_call | solution.py:383

commit v6 on v5

--- a/solution.py
+++ b/solution.py
@@ -10,7 +10,7 @@
 MESH = pl.DeviceIdType.MESH
 HALVES = 4
 GROUP = 8
-STEPS = 4
+STEPS = 2
 LEAD, SPACING = (-4.5, 0.0, 3.8, 5.0, 8.0), 9.6
 OFFSETS = ((0, 1), (1, 0), (3, 0), (2, 0), (1, 1), (3, 1), (2, 1))
 FREQ_OFFSETS = ((0, 1), (1, 1), (3, 1), (2, 1), (1, 0), (3, 0), (2, 0))

time: 46.1 us -> 46.4 us (level)
  no operation moved by 1% of the time
where the time goes in v6:
time: 46.4 us; the launch traced here: 46.3 us
  Pallas kernels  46.3 us (100%)
    pallas_call x1, Pallas kernels, on_device(): pl.pallas_call(exchange_kernel, out_shape=(jax.ShapeDtypeStruct((HALVES,...  40.2 us
    pallas_call x1, Pallas kernels, on_device(): pl.pallas_call(window_kernel, out_shape=jax.ShapeDtypeStruct((times, foca...  6.13 us

profile of v6, /device:TPU:1, one launch (start us, length us, event | category | flops | bytes accessed | tf_op | source)
XLA Modules:
  0.0 46.3 jit_solution(9634243213163413536)
XLA Ops:
  0.0 40.2 %exchange.1 = (bf16[4,8,2,2,2,8,256]{6,5,4,3,2,1,0:T(8,128)(2,1)}, bf16[2048,256]{1,0:T(8,128)(2,1)}) custom-call(bf16[256,64,256]{2,1,0:T(8,128)(2,1)} %traces.1, bf16[2,2,256,4096]{3,2,1,0:T(8,128)(2,1)} %reflection.1), custom_call_target="tpu_custom_call" | custom-call | tf_op jit(solution)/shard_map/exchange/pallas_call | solution.py:347
  40.2 6.1 %window.1 = bf16[256,64,256]{2,1,0:T(8,128)(2,1)} custom-call(bf16[2048,256]{1,0:T(8,128)(2,1)} %get-tuple-element.7.table, bf16[4,8,2,2,2,8,256]{6,5,4,3,2,1,0:T(8,128)(2,1)} %get-tuple-element.8.pieces, s32[64,256]{1,0:T(8,128)} %onset.1), custom_call_target="tpu_custom_call" | custom-call | tf_op jit(solution)/shard_map/window/pallas_call | solution.py:383
